TPU v7x, 32 devices: a whole 2x2x4 slice. The times are simulated.
32 devices in a mesh: groups: 2 (over x), row: 4 (over y, core), col: 4 (over z).
Axes of the slice: x: 2, y: 2, z: 4, core: 2. Of those that a mesh axis runs over, the one named last changes fastest.
Arguments:
- positions: float32 [3, 32768], P(None, ('groups', 'row', 'col')), parts along dimension 1, may hold values from -6 to 6
- strengths: float32 [3, 32768], P(None, ('groups', 'row', 'col')), parts along dimension 1, may hold values from -6 to 6
- cores: float32 [32768], P(('groups', 'row', 'col')), parts along dimension 0, may hold values from 0.3 to 1
- order: int32 [32768], P(('groups', 'row', 'col')), parts along dimension 0, may hold values from 0 to 1023, as said below
- tile_counts: int32 [256], P(('groups', 'row', 'col')), parts along dimension 0, may hold values from 32 to 128
- pair_slots: int32 [2, 2048], P(None, ('groups', 'row', 'col')), parts along dimension 1, may hold values from 0 to 31, as said below
- pair_count: int32 [32], P(('groups', 'row', 'col')), parts along dimension 0, may hold values from 16 to 64, as said below
Outputs:
- velocity: float32 [3, 32768], P(None, ('groups', 'row', 'col')), parts along dimension 1
- stretching: float32 [3, 32768], P(None, ('groups', 'row', 'col')), parts along dimension 1
There are 2 independent parts, one for each index of `groups`. A program takes and returns all parts, laid end to end along the dimension named above; each array names one. Nothing has to cross between parts.
Inputs may be any that keep to these rules, and one draw needn't show every extreme that they name: `order`: each device's block of 1024 entries is a permutation of 0 to 1023. `pair_slots`: row 0 is below 32, row 1 below 32; the first 8 slots of every device pair each of its own tiles with itself. `pair_count`: some device has all its slots live.
All inputs are finite; a program needn't handle non-finite values.
Results may differ from a plain program's by a relative error of at most 0.0001.
Values sent between devices are 32-bit elements; how exact they have to be, the bound alone decides.
A program may use at most 64 MiB of HBM per device.

v0:
```python
import functools
import math

import jax
import jax.numpy as jnp
from jax import lax
from jax.experimental import pallas as pl
from jax.experimental.pallas import tpu as pltpu
from jax.sharding import PartitionSpec as P

TILE = 128
MESH = pl.DeviceIdType.MESH
VMEM = pl.BlockSpec(memory_space=pltpu.VMEM)
SMEM = pl.BlockSpec(memory_space=pltpu.SMEM)
HBM = pl.BlockSpec(memory_space=pltpu.HBM)
UNROLL = 14
CHUNK = 16

biot_factor = -1.0 / (4.0 * math.pi)


def peers(nrows, ncols):
    return [("col", k) for k in range(1, ncols)] + [("row", k) for k in range(1, nrows)]


def greet(nrows, ncols):
    barrier = pltpu.get_barrier_semaphore()
    for axis, k in peers(nrows, ncols):
        size = ncols if axis == "col" else nrows
        other = lax.rem(lax.axis_index(axis) + k, size)
        pl.semaphore_signal(barrier, inc=1, device_id={axis: other}, device_id_type=MESH)
    return barrier


def split(value):
    high = value.astype(jnp.bfloat16)
    return high, (value - high.astype(jnp.float32)).astype(jnp.bfloat16)


def cross(left, right):
    return [left[(k + 1) % 3] * right[(k + 2) % 3] - left[(k + 2) % 3] * right[(k + 1) % 3] for k in range(3)]


def wake_kernel(nrows, ncols, tiles, slots, count, counts, slot_rows_in, pos_in, strg_in, cores_in, order_in,
                sums_out, slot_rows, pos, strg, cores, order, raw, row_blk, col_blk, spread, ones, stage, row_w, col_w, tgt_buf, src_buf,
                tgt_terms, src_terms, row_sum, col_sum, row_held, col_held, load, send, recv):
    pairs_in = [(pos_in, pos), (strg_in, strg), (cores_in, cores), (order_in, order), (slot_rows_in, slot_rows)]
    loads = [pltpu.make_async_copy(src, dst, load.at[n]) for n, (src, dst) in enumerate(pairs_in)]
    for copy in loads:
        copy.start()
    barrier = greet(nrows, ncols)
    row = lax.axis_index("row")
    col = lax.axis_index("col")
    num_slots = slot_rows.shape[1]
    lane = lax.broadcasted_iota(jnp.int32, (8, TILE), 1)
    sub = lax.broadcasted_iota(jnp.int32, (8, TILE), 0)
    own_row = pl.multiple_of(col * tiles, tiles)
    own_col = pl.multiple_of(row * tiles, tiles)

    stage[...] = jnp.zeros_like(stage)
    rank = lax.broadcasted_iota(jnp.int32, (16, TILE), 0)
    for k in range(3):
        ones[:, k * TILE : (k + 1) * TILE] = jnp.where((rank == k) | (rank == 6 + k), 1.0, 0.0).astype(jnp.bfloat16)
    ones[:, 3 * TILE :] = jnp.where((rank > 11) & (rank < 15), 1.0, 0.0).astype(jnp.bfloat16)
    for copy in loads:
        copy.wait()
    for t in range(tiles):
        part = slice(t * TILE, (t + 1) * TILE)
        raw[t, 0:3, :] = pos[:, part]
        raw[t, 3:6, :] = strg[:, part]
        raw[t, 6:7, :] = cores[t : t + 1, :]
        raw[t, 7:8, :] = cores[t : t + 1, :]
    for t in range(tiles):
        spot = jnp.broadcast_to(order[t : t + 1, :], (8, TILE))
        inner = spot & (TILE - 1)
        outer = spot >> 7
        found = jnp.zeros((8, TILE), jnp.float32)
        for s in range(tiles):
            found = jnp.where(outer == s, jnp.take_along_axis(raw[s], inner, axis=1), found)
        keep = (lane < counts[t]) | (sub < 3) | (sub > 5)
        found = jnp.where(keep, found, 0.0)
        row_blk[own_row + t] = found
        col_blk[own_col + t] = found

    pl.semaphore_wait(barrier, nrows + ncols - 2)
    copies = []
    for n, (axis, k) in enumerate(peers(nrows, ncols)):
        size, me, block, at = (ncols, col, row_blk, own_row) if axis == "col" else (nrows, row, col_blk, own_col)
        copy = pltpu.make_async_remote_copy(
            src_ref=block.at[pl.ds(at, tiles)],
            dst_ref=block.at[pl.ds(at, tiles)],
            send_sem=send.at[0, n],
            recv_sem=recv.at[0, n],
            device_id={axis: lax.rem(me + k, size)},
            device_id_type=MESH,
        )
        copy.start()
        copies.append(copy)

    def weights(block, at, out):
        some = block.at[pl.ds(at, tiles)]
        x = [some[:, k, :] for k in range(3)]
        a = [some[:, 3 + k, :] for k in range(3)]
        for k, value in enumerate(a + cross(x, a)):
            high = value.astype(jnp.bfloat16).astype(jnp.float32)
            stage[:, k, :] = high
            stage[:, 6 + k, :] = value - high
        sigma = some[:, 6, :]
        rest = 0.5 * sigma * sigma
        for k in range(3):
            high = rest.astype(jnp.bfloat16).astype(jnp.float32)
            stage[:, 12 + k, :] = high
            rest = rest - high
        for t in range(tiles):
            both = stage[t].astype(jnp.bfloat16)
            out[at + t, :, 0:TILE] = both
            out[at + t, :, TILE:] = both

    def prepare_row(k):
        at = pl.multiple_of(lax.rem(col + ncols - k, ncols) * tiles, tiles)
        weights(row_blk, at, row_w)
        for t in range(tiles):
            column = row_blk[at + t].T
            for j in range(3):
                spread[at + t, j] = jnp.broadcast_to(column[:, j : j + 1], (TILE, TILE))
            rest = lax.dot_general(row_w[at + t, :, 0:TILE], ones[...], (((0,), (0,)), ((), ())),
                                   preferred_element_type=jnp.float32)
            for j in range(4):
                spread[at + t, 3 + j] = rest[:, j * TILE : (j + 1) * TILE]

    def prepare_col(k):
        weights(col_blk, pl.multiple_of(lax.rem(row + nrows - k, nrows) * tiles, tiles), col_w)

    def pair(u, s, ti, sj, react):
        src = col_blk[sj]
        xj = [src[k : k + 1, :] for k in range(7)]
        hj = 0.5 * xj[6] * xj[6]
        for c in range(TILE // CHUNK):
            at = slice(c * CHUNK, (c + 1) * CHUNK)
            at2 = slice(TILE + c * CHUNK, TILE + (c + 1) * CHUNK)
            xi = [spread[ti, k, at, :] for k in range(7)]
            dx = xi[0] - xj[0]
            dy = xi[1] - xj[1]
            dz = xi[2] - xj[2]
            s2 = xi[6] + hj
            d = dx * dx + dy * dy + dz * dz + s2
            inv = lax.rsqrt(d)
            inv2 = inv * inv
            inv3 = inv2 * inv
            w = s2 * (inv3 * inv2)
            q = inv3 + 1.5 * w
            f = (q + w) * inv2
            g = f * (xi[3] * dx + xi[4] * dy + xi[5] * dz)
            q1, q2 = split(q)
            g1, g2 = split(g)
            tgt_buf[u, at, 0:TILE] = q1
            tgt_buf[u, at, TILE:] = q2
            tgt_buf[u, at2, 0:TILE] = g1
            tgt_buf[u, at2, TILE:] = g2
            if react:
                h = f * (xj[3] * dx + xj[4] * dy + xj[5] * dz)
                h1, h2 = split(h)
                src_buf[u, at, 0:TILE] = q1
                src_buf[u, at, TILE:] = h1
                src_buf[u, at2, 0:TILE] = q2
                src_buf[u, at2, TILE:] = h2
        out = lax.dot_general(col_w[sj], tgt_buf[u], (((1,), (1,)), ((), ())), preferred_element_type=jnp.float32)
        tgt_terms[s, 0:6, :] = out[0:6] + out[6:12]
        if react:
            out = lax.dot_general(row_w[ti], src_buf[u], (((1,), (0,)), ((), ())), preferred_element_type=jnp.float32)
            src_terms[s, 0:6, :] = out[0:6] + out[6:12]

    prepare_row(0)
    prepare_col(0)
    src_terms[0:tiles] = jnp.zeros((tiles, 8, 2 * TILE), jnp.float32)

    def diagonal(step, _):
        for u in range(4):
            t = step * 4 + u
            pair(u, t, own_row + t, own_col + t, False)
        return 0

    lax.fori_loop(0, tiles // 4, diagonal, 0)

    def arrived(axis, size, me, block, base, prepare):
        def step(k, _):
            other = lax.rem(me + size - k, size)
            place = block.at[pl.ds(pl.multiple_of(other * tiles, tiles), tiles)]
            pltpu.make_async_remote_copy(
                src_ref=place,
                dst_ref=place,
                send_sem=send.at[0, base + k - 1],
                recv_sem=recv.at[0, base + k - 1],
                device_id={axis: other},
                device_id_type=MESH,
            ).wait_recv()
            prepare(k)
            return 0

        lax.fori_loop(1, size, step, 0)

    arrived("col", ncols, col, row_blk, 0, prepare_row)
    arrived("row", nrows, row, col_blk, ncols - 1, prepare_col)

    def visit(step, _):
        for u in range(UNROLL):
            s = tiles + step * UNROLL + u
            pair(u, s, slots[0, s], slots[1, s], True)
        return 0

    lax.fori_loop(0, (num_slots - tiles) // UNROLL, visit, 0)

    first = slot_rows[0:1, :]
    second = slot_rows[1:2, :]
    slot = lax.broadcasted_iota(jnp.int32, (1, num_slots), 1)
    first = jnp.where(slot < tiles, own_row + slot, first)
    gi = row * (ncols * tiles) + first
    gj = ((second // tiles) * ncols + col) * tiles + second % tiles
    alive = slot < count[0]
    row_sel = jnp.where(alive, first, -1)
    col_sel = jnp.where(alive & (gi != gj) & (slot >= tiles), second, -1)

    def finish(select, terms, block, out, sign):
        size = block.shape[0]
        here = lax.broadcasted_iota(jnp.int32, (size, num_slots), 0)
        hot = jnp.where(here == select, 1.0, 0.0).astype(jnp.bfloat16)
        qs, fs = [], []
        for k in range(6):
            high, low = split(terms[:, k, :])
            value = jnp.dot(hot, high, preferred_element_type=jnp.float32)
            value += jnp.dot(hot, low, preferred_element_type=jnp.float32)
            qs.append(value[:, 0:TILE])
            fs.append(value[:, TILE:])
        x = [block[:, k, :] for k in range(3)]
        a = [block[:, 3 + k, :] for k in range(3)]
        velocity = cross(x, qs[0:3])
        turn = cross(a, qs[0:3])
        steep = cross(x, fs[0:3])
        for k in range(3):
            v = biot_factor * (velocity[k] - qs[3 + k])
            w = biot_factor * (turn[k] - (3.0 * sign) * (steep[k] - fs[3 + k]))
            out[:, k] = v.reshape(size // tiles, tiles, TILE)
            out[:, 3 + k] = w.reshape(size // tiles, tiles, TILE)

    for copy in copies:
        copy.wait_send()

    def send_all(axis, first_sem, size, me, sums, held):
        started = []
        for k in range(1, size):
            other = lax.rem(me + k, size)
            copy = pltpu.make_async_remote_copy(
                src_ref=sums.at[other],
                dst_ref=held.at[k - 1],
                send_sem=send.at[1, first_sem + k - 1],
                recv_sem=recv.at[1, first_sem + k - 1],
                device_id={axis: other},
                device_id_type=MESH,
            )
            copy.start()
            started.append((copy, held.at[k - 1]))
        return started

    finish(row_sel, tgt_terms, row_blk, row_sum, 1.0)
    started = send_all("col", 0, ncols, col, row_sum, row_held)
    finish(col_sel, src_terms, col_blk, col_sum, -1.0)
    started += send_all("row", ncols - 1, nrows, row, col_sum, col_held)
    total = row_sum[col] + col_sum[row]
    for copy, held in started:
        copy.wait_recv()
        total = total + held[...]
    for t in range(tiles):
        part = slice(t * TILE, (t + 1) * TILE)
        live = lane[0:1, :] < counts[t]
        for k in range(3):
            sums_out[k : k + 1, part] = jnp.where(live, total[k, t : t + 1, :], 0.0)
            sums_out[3 + k : 4 + k, part] = jnp.where(live, total[3 + k, t : t + 1, :], 0.0)
    for copy, _ in started:
        copy.wait_send()


def shards(nrows, ncols, positions, strengths, cores, order, tile_counts, pair_slots, pair_count):
    tiles = tile_counts.shape[0]
    num_slots = pair_slots.shape[1]
    others = nrows + ncols - 2
    nt, ns = ncols * tiles, nrows * tiles
    f32, bf16 = jnp.float32, jnp.bfloat16
    sums = pl.pallas_call(
        functools.partial(wake_kernel, nrows, ncols, tiles),
        out_shape=jax.ShapeDtypeStruct((6, tiles * TILE), f32),
        in_specs=[SMEM, SMEM, SMEM, HBM, HBM, HBM, HBM, HBM],
        out_specs=VMEM,
        scratch_shapes=[
            pltpu.VMEM((2, num_slots), jnp.int32),
            pltpu.VMEM((3, tiles * TILE), f32),
            pltpu.VMEM((3, tiles * TILE), f32),
            pltpu.VMEM((tiles, TILE), f32),
            pltpu.VMEM((tiles, TILE), jnp.int32),
            pltpu.VMEM((tiles, 8, TILE), f32),
            pltpu.VMEM((nt, 8, TILE), f32),
            pltpu.VMEM((ns, 8, TILE), f32),
            pltpu.VMEM((nt, 7, TILE, TILE), f32),
            pltpu.VMEM((16, 4 * TILE), bf16),
            pltpu.VMEM((tiles, 16, TILE), f32),
            pltpu.VMEM((nt, 16, 2 * TILE), bf16),
            pltpu.VMEM((ns, 16, 2 * TILE), bf16),
            pltpu.VMEM((UNROLL, 2 * TILE, 2 * TILE), bf16),
            pltpu.VMEM((UNROLL, 2 * TILE, 2 * TILE), bf16),
            pltpu.VMEM((num_slots, 8, 2 * TILE), f32),
            pltpu.VMEM((num_slots, 8, 2 * TILE), f32),
            pltpu.VMEM((ncols, 6, tiles, TILE), f32),
            pltpu.VMEM((nrows, 6, tiles, TILE), f32),
            pltpu.VMEM((ncols - 1, 6, tiles, TILE), f32),
            pltpu.VMEM((nrows - 1, 6, tiles, TILE), f32),
            pltpu.SemaphoreType.DMA((5,)),
            pltpu.SemaphoreType.DMA((2, others)),
            pltpu.SemaphoreType.DMA((2, others)),
        ],
        compiler_params=pltpu.CompilerParams(
            collective_id=0, has_side_effects=True, vmem_limit_bytes=56 * 1024 * 1024
        ),
        name="wake",
    )(pair_slots, pair_count, tile_counts, pair_slots, positions, strengths,
      cores.reshape(tiles, TILE), order.reshape(tiles, TILE))
    return sums[0:3], sums[3:6]


def solution(mesh):
    whole = ("groups", "row", "col")
    in_specs = (P(None, whole), P(None, whole), P(whole), P(whole), P(whole), P(None, whole), P(whole))
    out_specs = (P(None, whole), P(None, whole))
    body = functools.partial(shards, mesh.shape["row"], mesh.shape["col"])
    return jax.shard_map(body, mesh=mesh, in_specs=in_specs, out_specs=out_specs, check_vma=False)
```

profile of v0, /device:TPU:0, one launch (start us, length us, event | category | flops | bytes accessed | tf_op | source)
XLA Modules:
  0.0 27.0 jit_solution(5332338676541300161)
XLA Ops:
  1.3 24.3 %wake.1 = f32[6,1024]{1,0:T(8,128)} custom-call(s32[2,64]{1,0:T(2,128)} %slot_rows_in.1, s32[1]{0:T(128)S(6)} %copy.9.count, s32[8]{0:T(128)} %counts.1, s32[2,64]{1,0:T(2,128)} %slot_rows_in.1, f32[3,1024]{1,0:T(4,128)} %pos_in.1, f32[3,1024]{1,0:T(4,128)} %strg_in.1, f32[8,128]{1,0:T(8,128)} %bitcast.2, s32[8,128]{1,0:T(8,128)} %bitcast.3), custom_call_target="tpu_custom_call" | custom-call | tf_op jit(solution)/shard_map/wake/pallas_call | solution.py:288
  25.6 1.5 %fusion = (f32[3,1024]{1,0:T(4,128)}, f32[3,1024]{1,0:T(4,128)}) fusion(f32[6,1024]{1,0:T(8,128)} %wake.1), kind=kLoop, calls=%fused_computation | loop fusion | bytes 49152 | tf_op jit(solution)/shard_map/slice | solution.py:325
where the time goes:
time: 27.3 us; the launch traced here: 27 us
  Pallas kernels  24.3 us (89%)
  local copies, waits for them, and re-layouts  1.45 us (5%)
  between operations  1.29 us (5%)
    pallas_call x1, Pallas kernels, shards(): pl.pallas_call(functools.partial(wake_kernel, nrows, ncols, tiles), out_s...  24.3 us
    slice x1, local copies, waits for them, and re-layouts, shards(): return (sums[0:3], sums[3:6])  1.45 us

commit v1 on v0

--- a/solution.py
+++ b/solution.py
@@ -41,14 +41,15 @@
     return [left[(k + 1) % 3] * right[(k + 2) % 3] - left[(k + 2) % 3] * right[(k + 1) % 3] for k in range(3)]
 
 
-def wake_kernel(nrows, ncols, tiles, slots, count, counts, slot_rows_in, pos_in, strg_in, cores_in, order_in,
-                sums_out, slot_rows, pos, strg, cores, order, raw, row_blk, col_blk, spread, ones, stage, row_w, col_w, tgt_buf, src_buf,
+def wake_kernel(nrows, ncols, tiles, count_in, counts_in, slots_in, pos_in, strg_in, cores_in, order_in,
+                sums_out, slots, count, counts, slot_rows, pos, strg, cores, order, raw, row_blk, col_blk, spread, ones, stage, row_w, col_w, tgt_buf, src_buf,
                 tgt_terms, src_terms, row_sum, col_sum, row_held, col_held, load, send, recv):
-    pairs_in = [(pos_in, pos), (strg_in, strg), (cores_in, cores), (order_in, order), (slot_rows_in, slot_rows)]
+    barrier = greet(nrows, ncols)
+    pairs_in = [(pos_in, pos), (strg_in, strg), (cores_in, cores), (order_in, order), (counts_in, counts),
+                (slots_in, slot_rows), (slots_in, slots), (count_in, count)]
     loads = [pltpu.make_async_copy(src, dst, load.at[n]) for n, (src, dst) in enumerate(pairs_in)]
     for copy in loads:
         copy.start()
-    barrier = greet(nrows, ncols)
     row = lax.axis_index("row")
     col = lax.axis_index("col")
     num_slots = slot_rows.shape[1]
@@ -287,10 +288,13 @@
     f32, bf16 = jnp.float32, jnp.bfloat16
     sums = pl.pallas_call(
         functools.partial(wake_kernel, nrows, ncols, tiles),
-        out_shape=jax.ShapeDtypeStruct((6, tiles * TILE), f32),
-        in_specs=[SMEM, SMEM, SMEM, HBM, HBM, HBM, HBM, HBM],
+        out_shape=pltpu.VMEM((6, tiles * TILE), f32),
+        in_specs=[HBM] * 7,
         out_specs=VMEM,
         scratch_shapes=[
+            pltpu.SMEM((2, num_slots), jnp.int32),
+            pltpu.SMEM((1,), jnp.int32),
+            pltpu.SMEM((tiles,), jnp.int32),
             pltpu.VMEM((2, num_slots), jnp.int32),
             pltpu.VMEM((3, tiles * TILE), f32),
             pltpu.VMEM((3, tiles * TILE), f32),
@@ -312,7 +316,7 @@
             pltpu.VMEM((nrows, 6, tiles, TILE), f32),
             pltpu.VMEM((ncols - 1, 6, tiles, TILE), f32),
             pltpu.VMEM((nrows - 1, 6, tiles, TILE), f32),
-            pltpu.SemaphoreType.DMA((5,)),
+            pltpu.SemaphoreType.DMA((8,)),
             pltpu.SemaphoreType.DMA((2, others)),
             pltpu.SemaphoreType.DMA((2, others)),
         ],
@@ -320,7 +324,7 @@
             collective_id=0, has_side_effects=True, vmem_limit_bytes=56 * 1024 * 1024
         ),
         name="wake",
-    )(pair_slots, pair_count, tile_counts, pair_slots, positions, strengths,
+    )(pair_count, tile_counts, pair_slots, positions, strengths,
       cores.reshape(tiles, TILE), order.reshape(tiles, TILE))
     return sums[0:3], sums[3:6]
 

time: 27.3 us -> 25.4 us (0.930)
  Pallas kernels: 24.3 us -> 23.2 us
  local copies, waits for them, and re-layouts: 1.45 us -> 0.62 us
    pallas_call x1, Pallas kernels: 24.3 us -> 23.2 us  [shards(): pl.pallas_call(functools.partial(wake_kernel, nrows, ncols, tiles), out_s...]
    slice x1, local copies, waits for them, and re-layouts: 1.45 us -> 0.62 us  [shards(): return (sums[0:3], sums[3:6])]
where the time goes in v1:
time: 25.4 us; the launch traced here: 25.1 us
  Pallas kernels  23.2 us (91%)
  between operations  1.29 us (5%)
  local copies, waits for them, and re-layouts  0.62 us (2%)
    pallas_call x1, Pallas kernels, shards(): pl.pallas_call(functools.partial(wake_kernel, nrows, ncols, tiles), out_s...  23.2 us
    slice x1, local copies, waits for them, and re-layouts, shards(): return (sums[0:3], sums[3:6])  0.62 us

profile of v1, /device:TPU:0, one launch (start us, length us, event | category | flops | bytes accessed | tf_op | source)
XLA Modules:
  0.0 25.1 jit_solution(8112463919577880374)
XLA Ops:
  1.3 23.2 %wake.1 = f32[6,1024]{1,0:T(8,128)S(1)} custom-call(s32[1]{0:T(128)S(6)} %copy.9.count_in, s32[8]{0:T(128)} %counts_in.1, s32[2,64]{1,0:T(2,128)} %slots_in.1, f32[3,1024]{1,0:T(4,128)} %pos_in.1, f32[3,1024]{1,0:T(4,128)} %strg_in.1, f32[8,128]{1,0:T(8,128)} %bitcast.2, s32[8,128]{1,0:T(8,128)} %bitcast.3), custom_call_target="tpu_custom_call" | custom-call | tf_op jit(solution)/shard_map/wake/pallas_call | solution.py:289
  24.5 0.6 %fusion = (f32[3,1024]{1,0:T(4,128)}, f32[3,1024]{1,0:T(4,128)}) fusion(f32[6,1024]{1,0:T(8,128)S(1)} %wake.1), kind=kLoop, calls=%fused_computation | loop fusion | bytes 49152 | tf_op jit(solution)/shard_map/slice | solution.py:329

commit v2 on v1

v2 whole, which is shorter than its diff:
```python
import functools
import math

import jax
import jax.numpy as jnp
from jax import lax
from jax.experimental import pallas as pl
from jax.experimental.pallas import tpu as pltpu
from jax.sharding import PartitionSpec as P

TILE = 128
MESH = pl.DeviceIdType.MESH
VMEM = pl.BlockSpec(memory_space=pltpu.VMEM)
SMEM = pl.BlockSpec(memory_space=pltpu.SMEM)
HBM = pl.BlockSpec(memory_space=pltpu.HBM)
UNROLL = 14
CHUNK = 16
MOMENTS = 24
WROWS = 80
FROWS = 32
PLANES = 32

biot_factor = -1.0 / (4.0 * math.pi)


def peers(nrows, ncols):
    return [("col", k) for k in range(1, ncols)] + [("row", k) for k in range(1, nrows)]


def greet(nrows, ncols):
    barrier = pltpu.get_barrier_semaphore()
    for axis, k in peers(nrows, ncols):
        size = ncols if axis == "col" else nrows
        other = lax.rem(lax.axis_index(axis) + k, size)
        pl.semaphore_signal(barrier, inc=1, device_id={axis: other}, device_id_type=MESH)
    return barrier


def split(value):
    high = value.astype(jnp.bfloat16)
    return high, (value - high.astype(jnp.float32)).astype(jnp.bfloat16)


def thirds(value):
    first = value.astype(jnp.bfloat16).astype(jnp.float32)
    rest = value - first
    second = rest.astype(jnp.bfloat16).astype(jnp.float32)
    return first, second, rest - second


def cross(left, right):
    return [left[(k + 1) % 3] * right[(k + 2) % 3] - left[(k + 2) % 3] * right[(k + 1) % 3] for k in range(3)]


def dot3(left, right):
    return left[0] * right[0] + left[1] * right[1] + left[2] * right[2]


def wake_kernel(nrows, ncols, tiles, count_in, counts_in, slots_in, pos_in, strg_in, cores_in, order_in,
                sums_out, slots, count, counts, slot_rows, pos, strg, cores, order, raw, row_blk, col_blk, center,
                stage, row_near, col_near, col_wide, row_w, col_w, row_f, col_f, near_buf, tgt_buf, src_buf,
                tgt_terms, src_terms, row_sum, col_sum, row_held, col_held, load, send, recv):
    barrier = greet(nrows, ncols)
    pairs_in = [(pos_in, pos), (strg_in, strg), (cores_in, cores), (order_in, order), (counts_in, counts),
                (slots_in, slot_rows), (slots_in, slots), (count_in, count)]
    loads = [pltpu.make_async_copy(src, dst, load.at[n]) for n, (src, dst) in enumerate(pairs_in)]
    for copy in loads:
        copy.start()
    row = lax.axis_index("row")
    col = lax.axis_index("col")
    num_slots = slot_rows.shape[1]
    lane = lax.broadcasted_iota(jnp.int32, (8, TILE), 1)
    sub = lax.broadcasted_iota(jnp.int32, (8, TILE), 0)

    for copy in loads:
        copy.wait()
    for t in range(tiles):
        part = slice(t * TILE, (t + 1) * TILE)
        raw[t, 0:3, :] = pos[:, part]
        raw[t, 3:6, :] = strg[:, part]
        raw[t, 6:7, :] = cores[t : t + 1, :]
        raw[t, 7:8, :] = cores[t : t + 1, :]
    for t in range(tiles):
        spot = jnp.broadcast_to(order[t : t + 1, :], (8, TILE))
        inner = spot & (TILE - 1)
        outer = spot >> 7
        found = jnp.zeros((8, TILE), jnp.float32)
        for s in range(tiles):
            found = jnp.where(outer == s, jnp.take_along_axis(raw[s], inner, axis=1), found)
        keep = (lane < counts[t]) | (sub < 3) | (sub > 5)
        found = jnp.where(keep, found, 0.0)
        own = pl.ds(t, 7, stride=tiles)
        row_blk[col, own, :] = found[0:7]
        col_blk[row, own, :] = found[0:7]

    pl.semaphore_wait(barrier, nrows + ncols - 2)
    copies = []
    for n, (axis, k) in enumerate(peers(nrows, ncols)):
        size, me, block = (ncols, col, row_blk) if axis == "col" else (nrows, row, col_blk)
        copy = pltpu.make_async_remote_copy(
            src_ref=block.at[me],
            dst_ref=block.at[me],
            send_sem=send.at[0, n],
            recv_sem=recv.at[0, n],
            device_id={axis: lax.rem(me + k, size)},
            device_id_type=MESH,
        )
        copy.start()
        copies.append(copy)

    for t in range(tiles):
        stage[t * WROWS + 3 * MOMENTS : (t + 1) * WROWS, :] = jnp.zeros((WROWS - 3 * MOMENTS, TILE), jnp.float32)
    rank = lax.rem(lax.broadcasted_iota(jnp.int32, (tiles * FROWS, TILE), 0), FROWS)
    row_near[...] = jnp.where((rank > 20) & (rank < 24), 1.0, 0.0)
    col_near[...] = jnp.where((rank > 17) & (rank < 21), 1.0, 0.0)
    col_wide[...] = jnp.where((rank > 23) & (rank < 27), 1.0, 0.0)
    for plane in range(PLANES):
        src_terms[plane * num_slots : plane * num_slots + tiles, :] = jnp.zeros((tiles, TILE), jnp.float32)
    for k in range(3):
        mean = jnp.sum(row_blk[col, k * tiles : (k + 1) * tiles], keepdims=True) * (1.0 / (tiles * TILE))
        center[k] = jnp.broadcast_to(mean, (tiles, TILE))

    def part(block, at, k):
        return block[at, k * tiles : (k + 1) * tiles]

    def put(out, rows, r, value):
        out[pl.ds(r, tiles, stride=rows), :] = value

    def prepare(block, at, weights, near, wide_near, features, target):
        x = [part(block, at, k) - center[k] for k in range(3)]
        a = [part(block, at, 3 + k) for k in range(3)]
        b = cross(x, a)
        moments = a + b + [p * v for p in x for v in a] + [p * v for p in x for v in b]
        for r, value in enumerate(moments):
            for j, piece in enumerate(thirds(value)):
                put(stage, WROWS, j * MOMENTS + r, piece)
        sigma = part(block, at, 6)
        half = 0.5 * sigma * sigma
        norm = thirds(dot3(x, x) + half)
        wide = thirds(1.5 * half)
        places = [thirds(value if target else -2.0 * value) for value in x]
        for n, j in enumerate((0, 0, 0, 1, 1, 2) if target else (0, 1, 2, 0, 1, 0)):
            for k in range(3):
                put(near, FROWS, 3 * n + k, places[k][j])
        for j in range(3):
            put(near, FROWS, (18 if target else 21) + j, norm[j])
            put(wide_near, FROWS, (24 if target else 21) + j, wide[j])
        for t in range(tiles):
            weights[at * tiles + t] = stage[t * WROWS : (t + 1) * WROWS, :].astype(jnp.bfloat16)
            some = slice(t * FROWS, (t + 1) * FROWS)
            features[at * tiles + t, :, 0:TILE] = near[some, :].astype(jnp.bfloat16)
            if not target:
                features[at * tiles + t, :, TILE:] = wide_near[some, :].astype(jnp.bfloat16)

    def prepare_row(k):
        prepare(row_blk, lax.rem(col + ncols - k, ncols), row_w, row_near, row_near, row_f, True)

    def prepare_col(k):
        prepare(col_blk, lax.rem(row + nrows - k, nrows), col_w, col_near, col_wide, col_f, False)

    def keep_terms(terms, s, out):
        for n, (first, at) in enumerate(((0, 0), (0, TILE), (8, TILE), (16, TILE))):
            total = out[first : first + 8, at : at + TILE]
            for j in (1, 2):
                total = total + out[j * MOMENTS + first : j * MOMENTS + first + 8, at : at + TILE]
            terms[pl.ds(n * 8 * num_slots + s, 8, stride=num_slots), :] = total

    def meet(u, ti, sj):
        near_buf[u] = lax.dot_general(row_f[ti], col_f[sj], (((0,), (0,)), ((), ())), preferred_element_type=jnp.float32)

    def spread(u, react):
        near = near_buf[u]
        for c in range(TILE // CHUNK):
            at = slice(c * CHUNK, (c + 1) * CHUNK)
            at2 = slice(TILE + c * CHUNK, TILE + (c + 1) * CHUNK)
            inv = lax.rsqrt(near[at, 0:TILE])
            inv2 = inv * inv
            ratio = near[at, TILE:] * inv2
            inv3 = inv2 * inv
            q1, q2 = split(inv3 * (ratio + 1.0))
            f1, f2 = split((inv3 * inv2) * (ratio + 0.6))
            tgt_buf[u, at, 0:TILE] = q1
            tgt_buf[u, at, TILE:] = q2
            tgt_buf[u, at2, 0:TILE] = f1
            tgt_buf[u, at2, TILE:] = f2
            if react:
                src_buf[u, at, 0:TILE] = q1
                src_buf[u, at, TILE:] = f1
                src_buf[u, at2, 0:TILE] = q2
                src_buf[u, at2, TILE:] = f2

    def gather(u, s, ti, sj, react):
        some = col_w[sj]
        both = jnp.concatenate([some, some], axis=1)
        out = lax.dot_general(both, tgt_buf[u], (((1,), (1,)), ((), ())), preferred_element_type=jnp.float32)
        keep_terms(tgt_terms, s, out)
        if react:
            some = row_w[ti]
            both = jnp.concatenate([some, some], axis=1)
            out = lax.dot_general(both, src_buf[u], (((1,), (0,)), ((), ())), preferred_element_type=jnp.float32)
            keep_terms(src_terms, s, out)

    def group(places, react):
        for u, (s, ti, sj) in enumerate(places):
            meet(u, ti, sj)
        for u, (s, ti, sj) in enumerate(places):
            spread(u, react)
        for u, (s, ti, sj) in enumerate(places):
            gather(u, s, ti, sj, react)

    prepare_row(0)
    prepare_col(0)

    def diagonal(step, _):
        places = [(step * 4 + u, col * tiles + step * 4 + u, row * tiles + step * 4 + u) for u in range(4)]
        group(places, False)
        return 0

    lax.fori_loop(0, tiles // 4, diagonal, 0)

    def arrived(axis, size, me, block, base, prepare_one):
        def step(k, _):
            other = lax.rem(me + size - k, size)
            place = block.at[other]
            pltpu.make_async_remote_copy(
                src_ref=place,
                dst_ref=place,
                send_sem=send.at[0, base + k - 1],
                recv_sem=recv.at[0, base + k - 1],
                device_id={axis: other},
                device_id_type=MESH,
            ).wait_recv()
            prepare_one(k)
            return 0

        lax.fori_loop(1, size, step, 0)

    arrived("col", ncols, col, row_blk, 0, prepare_row)
    arrived("row", nrows, row, col_blk, ncols - 1, prepare_col)

    def visit(step, _):
        first = tiles + step * UNROLL
        group([(first + u, slots[0, first + u], slots[1, first + u]) for u in range(UNROLL)], True)
        return 0

    lax.fori_loop(0, (num_slots - tiles) // UNROLL, visit, 0)

    first = slot_rows[0:1, :]
    second = slot_rows[1:2, :]
    slot = lax.broadcasted_iota(jnp.int32, (1, num_slots), 1)
    first = jnp.where(slot < tiles, col * tiles + slot, first)
    gi = row * (ncols * tiles) + first
    gj = ((second // tiles) * ncols + col) * tiles + second % tiles
    alive = slot < count[0]
    row_sel = jnp.where(alive, first, -1)
    col_sel = jnp.where(alive & (gi != gj) & (slot >= tiles), second, -1)

    def finish(select, terms, block, out):
        size = block.shape[0] * tiles
        here = lax.broadcasted_iota(jnp.int32, (size, num_slots), 0)
        hot = jnp.where(here == select, 1.0, 0.0)
        hot = jnp.concatenate([hot, hot, hot], axis=1).astype(jnp.bfloat16)
        sums = []
        for n in range(PLANES // 2):
            pieces = [thirds(terms[(2 * n + m) * num_slots : (2 * n + m + 1) * num_slots, :]) for m in range(2)]
            rows = jnp.concatenate([jnp.concatenate([pieces[0][j], pieces[1][j]], axis=1) for j in range(3)], axis=0)
            value = jnp.dot(hot, rows.astype(jnp.bfloat16), preferred_element_type=jnp.float32)
            sums += [value[:, 0:TILE], value[:, TILE:]]
        qa, qb, fa, fb = sums[0:3], sums[3:6], sums[8:11], sums[11:14]
        fxa, fxb = sums[14:23], sums[23:32]
        x = [block[:, k * tiles : (k + 1) * tiles].reshape(size, TILE) - center[k, 0:1] for k in range(3)]
        a = [block[:, (3 + k) * tiles : (4 + k) * tiles].reshape(size, TILE) for k in range(3)]
        velocity = cross(x, qa)
        turn = cross(a, qa)
        along = dot3(a, x)
        spin = cross(x, fa)
        toward = [dot3(a, [fxa[3 * k + m] for k in range(3)]) for m in range(3)]
        swing = cross(x, toward)
        for k in range(3):
            steep = along * (spin[k] - fb[k]) - swing[k] + dot3(a, [fxb[3 * m + k] for m in range(3)])
            v = biot_factor * (velocity[k] - qb[k])
            w = biot_factor * (turn[k] - 5.0 * steep)
            out[:, k] = v.reshape(size // tiles, tiles, TILE)
            out[:, 3 + k] = w.reshape(size // tiles, tiles, TILE)

    for copy in copies:
        copy.wait_send()

    def send_all(axis, first_sem, size, me, sums, held):
        started = []
        for k in range(1, size):
            other = lax.rem(me + k, size)
            copy = pltpu.make_async_remote_copy(
                src_ref=sums.at[other],
                dst_ref=held.at[k - 1],
                send_sem=send.at[1, first_sem + k - 1],
                recv_sem=recv.at[1, first_sem + k - 1],
                device_id={axis: other},
                device_id_type=MESH,
            )
            copy.start()
            started.append((copy, held.at[k - 1]))
        return started

    finish(row_sel, tgt_terms, row_blk, row_sum)
    started = send_all("col", 0, ncols, col, row_sum, row_held)
    finish(col_sel, src_terms, col_blk, col_sum)
    started += send_all("row", ncols - 1, nrows, row, col_sum, col_held)
    total = row_sum[col] + col_sum[row]
    for copy, held in started:
        copy.wait_recv()
        total = total + held[...]
    for t in range(tiles):
        part = slice(t * TILE, (t + 1) * TILE)
        live = lane[0:1, :] < counts[t]
        for k in range(3):
            sums_out[k : k + 1, part] = jnp.where(live, total[k, t : t + 1, :], 0.0)
            sums_out[3 + k : 4 + k, part] = jnp.where(live, total[3 + k, t : t + 1, :], 0.0)
    for copy, _ in started:
        copy.wait_send()


def shards(nrows, ncols, positions, strengths, cores, order, tile_counts, pair_slots, pair_count):
    tiles = tile_counts.shape[0]
    num_slots = pair_slots.shape[1]
    others = nrows + ncols - 2
    nt, ns = ncols * tiles, nrows * tiles
    f32, bf16 = jnp.float32, jnp.bfloat16
    sums = pl.pallas_call(
        functools.partial(wake_kernel, nrows, ncols, tiles),
        out_shape=pltpu.VMEM((6, tiles * TILE), f32),
        in_specs=[HBM] * 7,
        out_specs=VMEM,
        scratch_shapes=[
            pltpu.SMEM((2, num_slots), jnp.int32),
            pltpu.SMEM((1,), jnp.int32),
            pltpu.SMEM((tiles,), jnp.int32),
            pltpu.VMEM((2, num_slots), jnp.int32),
            pltpu.VMEM((3, tiles * TILE), f32),
            pltpu.VMEM((3, tiles * TILE), f32),
            pltpu.VMEM((tiles, TILE), f32),
            pltpu.VMEM((tiles, TILE), jnp.int32),
            pltpu.VMEM((tiles, 8, TILE), f32),
            pltpu.VMEM((ncols, 7 * tiles, TILE), f32),
            pltpu.VMEM((nrows, 7 * tiles, TILE), f32),
            pltpu.VMEM((3, tiles, TILE), f32),
            pltpu.VMEM((tiles * WROWS, TILE), f32),
            pltpu.VMEM((tiles * FROWS, TILE), f32),
            pltpu.VMEM((tiles * FROWS, TILE), f32),
            pltpu.VMEM((tiles * FROWS, TILE), f32),
            pltpu.VMEM((nt, WROWS, TILE), bf16),
            pltpu.VMEM((ns, WROWS, TILE), bf16),
            pltpu.VMEM((nt, FROWS, TILE), bf16),
            pltpu.VMEM((ns, FROWS, 2 * TILE), bf16),
            pltpu.VMEM((UNROLL, TILE, 2 * TILE), f32),
            pltpu.VMEM((UNROLL, 2 * TILE, 2 * TILE), bf16),
            pltpu.VMEM((UNROLL, 2 * TILE, 2 * TILE), bf16),
            pltpu.VMEM((PLANES * num_slots, TILE), f32),
            pltpu.VMEM((PLANES * num_slots, TILE), f32),
            pltpu.VMEM((ncols, 6, tiles, TILE), f32),
            pltpu.VMEM((nrows, 6, tiles, TILE), f32),
            pltpu.VMEM((ncols - 1, 6, tiles, TILE), f32),
            pltpu.VMEM((nrows - 1, 6, tiles, TILE), f32),
            pltpu.SemaphoreType.DMA((8,)),
            pltpu.SemaphoreType.DMA((2, others)),
            pltpu.SemaphoreType.DMA((2, others)),
        ],
        compiler_params=pltpu.CompilerParams(
            collective_id=0, has_side_effects=True, vmem_limit_bytes=56 * 1024 * 1024
        ),
        name="wake",
    )(pair_count, tile_counts, pair_slots, positions, strengths,
      cores.reshape(tiles, TILE), order.reshape(tiles, TILE))
    return sums[0:3], sums[3:6]


def solution(mesh):
    whole = ("groups", "row", "col")
    in_specs = (P(None, whole), P(None, whole), P(whole), P(whole), P(whole), P(None, whole), P(whole))
    out_specs = (P(None, whole), P(None, whole))
    body = functools.partial(shards, mesh.shape["row"], mesh.shape["col"])
    return jax.shard_map(body, mesh=mesh, in_specs=in_specs, out_specs=out_specs, check_vma=False)
```

time: 25.4 us -> 23.1 us (0.909)
  Pallas kernels: 23.2 us -> 21 us
    pallas_call x1, Pallas kernels: 23.2 us -> 21 us  [shards(): pl.pallas_call(functools.partial(wake_kernel, nrows, ncols, tiles), out_s...]
where the time goes in v2:
time: 23.1 us; the launch traced here: 22.9 us
  Pallas kernels  21 us (91%)
  between operations  1.29 us (6%)
  local copies, waits for them, and re-layouts  0.62 us (3%)
    pallas_call x1, Pallas kernels, shards(): pl.pallas_call(functools.partial(wake_kernel, nrows, ncols, tiles), out_s...  21 us
    slice x1, local copies, waits for them, and re-layouts, shards(): return (sums[0:3], sums[3:6])  0.62 us

profile of v2, /device:TPU:0, one launch (start us, length us, event | category | flops | bytes accessed | tf_op | source)
XLA Modules:
  0.0 22.9 jit_solution(18321738646631359203)
XLA Ops:
  1.3 21.0 %wake.1 = f32[6,1024]{1,0:T(8,128)S(1)} custom-call(s32[1]{0:T(128)S(6)} %copy.9.count_in, s32[8]{0:T(128)} %counts_in.1, s32[2,64]{1,0:T(2,128)} %slots_in.1, f32[3,1024]{1,0:T(4,128)} %pos_in.1, f32[3,1024]{1,0:T(4,128)} %strg_in.1, f32[8,128]{1,0:T(8,128)} %bitcast.2, s32[8,128]{1,0:T(8,128)} %bitcast.3), custom_call_target="tpu_custom_call" | custom-call | tf_op jit(solution)/shard_map/wake/pallas_call | solution.py:329
  22.3 0.6 %fusion = (f32[3,1024]{1,0:T(4,128)}, f32[3,1024]{1,0:T(4,128)}) fusion(f32[6,1024]{1,0:T(8,128)S(1)} %wake.1), kind=kLoop, calls=%fused_computation | loop fusion | bytes 49152 | tf_op jit(solution)/shard_map/slice | solution.py:374

commit v3 on v2

--- a/solution.py
+++ b/solution.py
@@ -17,7 +17,9 @@
 CHUNK = 16
 MOMENTS = 24
 WROWS = 80
+WPITCH = 84
 FROWS = 32
+FPITCH = 36
 PLANES = 32
 
 biot_factor = -1.0 / (4.0 * math.pi)
@@ -69,6 +71,7 @@
     row = lax.axis_index("row")
     col = lax.axis_index("col")
     num_slots = slot_rows.shape[1]
+    pitch = num_slots + 4
     lane = lax.broadcasted_iota(jnp.int32, (8, TILE), 1)
     sub = lax.broadcasted_iota(jnp.int32, (8, TILE), 0)
 
@@ -109,13 +112,13 @@
         copies.append(copy)
 
     for t in range(tiles):
-        stage[t * WROWS + 3 * MOMENTS : (t + 1) * WROWS, :] = jnp.zeros((WROWS - 3 * MOMENTS, TILE), jnp.float32)
-    rank = lax.rem(lax.broadcasted_iota(jnp.int32, (tiles * FROWS, TILE), 0), FROWS)
+        stage[t * WPITCH + 3 * MOMENTS : t * WPITCH + WROWS, :] = jnp.zeros((WROWS - 3 * MOMENTS, TILE), jnp.float32)
+    rank = lax.rem(lax.broadcasted_iota(jnp.int32, (tiles * FPITCH, TILE), 0), FPITCH)
     row_near[...] = jnp.where((rank > 20) & (rank < 24), 1.0, 0.0)
     col_near[...] = jnp.where((rank > 17) & (rank < 21), 1.0, 0.0)
     col_wide[...] = jnp.where((rank > 23) & (rank < 27), 1.0, 0.0)
     for plane in range(PLANES):
-        src_terms[plane * num_slots : plane * num_slots + tiles, :] = jnp.zeros((tiles, TILE), jnp.float32)
+        src_terms[plane * pitch : plane * pitch + tiles, :] = jnp.zeros((tiles, TILE), jnp.float32)
     for k in range(3):
         mean = jnp.sum(row_blk[col, k * tiles : (k + 1) * tiles], keepdims=True) * (1.0 / (tiles * TILE))
         center[k] = jnp.broadcast_to(mean, (tiles, TILE))
@@ -133,7 +136,7 @@
         moments = a + b + [p * v for p in x for v in a] + [p * v for p in x for v in b]
         for r, value in enumerate(moments):
             for j, piece in enumerate(thirds(value)):
-                put(stage, WROWS, j * MOMENTS + r, piece)
+                put(stage, WPITCH, j * MOMENTS + r, piece)
         sigma = part(block, at, 6)
         half = 0.5 * sigma * sigma
         norm = thirds(dot3(x, x) + half)
@@ -141,13 +144,13 @@
         places = [thirds(value if target else -2.0 * value) for value in x]
         for n, j in enumerate((0, 0, 0, 1, 1, 2) if target else (0, 1, 2, 0, 1, 0)):
             for k in range(3):
-                put(near, FROWS, 3 * n + k, places[k][j])
+                put(near, FPITCH, 3 * n + k, places[k][j])
         for j in range(3):
-            put(near, FROWS, (18 if target else 21) + j, norm[j])
-            put(wide_near, FROWS, (24 if target else 21) + j, wide[j])
+            put(near, FPITCH, (18 if target else 21) + j, norm[j])
+            put(wide_near, FPITCH, (24 if target else 21) + j, wide[j])
         for t in range(tiles):
-            weights[at * tiles + t] = stage[t * WROWS : (t + 1) * WROWS, :].astype(jnp.bfloat16)
-            some = slice(t * FROWS, (t + 1) * FROWS)
+            weights[at * tiles + t] = stage[t * WPITCH : t * WPITCH + WROWS, :].astype(jnp.bfloat16)
+            some = slice(t * FPITCH, t * FPITCH + FROWS)
             features[at * tiles + t, :, 0:TILE] = near[some, :].astype(jnp.bfloat16)
             if not target:
                 features[at * tiles + t, :, TILE:] = wide_near[some, :].astype(jnp.bfloat16)
@@ -163,7 +166,7 @@
             total = out[first : first + 8, at : at + TILE]
             for j in (1, 2):
                 total = total + out[j * MOMENTS + first : j * MOMENTS + first + 8, at : at + TILE]
-            terms[pl.ds(n * 8 * num_slots + s, 8, stride=num_slots), :] = total
+            terms[pl.ds(n * 8 * pitch + s, 8, stride=pitch), :] = total
 
     def meet(u, ti, sj):
         near_buf[u] = lax.dot_general(row_f[ti], col_f[sj], (((0,), (0,)), ((), ())), preferred_element_type=jnp.float32)
@@ -262,7 +265,7 @@
         hot = jnp.concatenate([hot, hot, hot], axis=1).astype(jnp.bfloat16)
         sums = []
         for n in range(PLANES // 2):
-            pieces = [thirds(terms[(2 * n + m) * num_slots : (2 * n + m + 1) * num_slots, :]) for m in range(2)]
+            pieces = [thirds(terms[(2 * n + m) * pitch : (2 * n + m) * pitch + num_slots, :]) for m in range(2)]
             rows = jnp.concatenate([jnp.concatenate([pieces[0][j], pieces[1][j]], axis=1) for j in range(3)], axis=0)
             value = jnp.dot(hot, rows.astype(jnp.bfloat16), preferred_element_type=jnp.float32)
             sums += [value[:, 0:TILE], value[:, TILE:]]
@@ -344,10 +347,10 @@
             pltpu.VMEM((ncols, 7 * tiles, TILE), f32),
             pltpu.VMEM((nrows, 7 * tiles, TILE), f32),
             pltpu.VMEM((3, tiles, TILE), f32),
-            pltpu.VMEM((tiles * WROWS, TILE), f32),
-            pltpu.VMEM((tiles * FROWS, TILE), f32),
-            pltpu.VMEM((tiles * FROWS, TILE), f32),
-            pltpu.VMEM((tiles * FROWS, TILE), f32),
+            pltpu.VMEM((tiles * WPITCH, TILE), f32),
+            pltpu.VMEM((tiles * FPITCH, TILE), f32),
+            pltpu.VMEM((tiles * FPITCH, TILE), f32),
+            pltpu.VMEM((tiles * FPITCH, TILE), f32),
             pltpu.VMEM((nt, WROWS, TILE), bf16),
             pltpu.VMEM((ns, WROWS, TILE), bf16),
             pltpu.VMEM((nt, FROWS, TILE), bf16),
@@ -355,8 +358,8 @@
             pltpu.VMEM((UNROLL, TILE, 2 * TILE), f32),
             pltpu.VMEM((UNROLL, 2 * TILE, 2 * TILE), bf16),
             pltpu.VMEM((UNROLL, 2 * TILE, 2 * TILE), bf16),
-            pltpu.VMEM((PLANES * num_slots, TILE), f32),
-            pltpu.VMEM((PLANES * num_slots, TILE), f32),
+            pltpu.VMEM((PLANES * (num_slots + 4), TILE), f32),
+            pltpu.VMEM((PLANES * (num_slots + 4), TILE), f32),
             pltpu.VMEM((ncols, 6, tiles, TILE), f32),
             pltpu.VMEM((nrows, 6, tiles, TILE), f32),
             pltpu.VMEM((ncols - 1, 6, tiles, TILE), f32),

time: 23.1 us -> 21.6 us (0.935)
  Pallas kernels: 21 us -> 19.5 us
    pallas_call x1, Pallas kernels: 21 us -> 19.5 us  [shards(): pl.pallas_call(functools.partial(wake_kernel, nrows, ncols, tiles), out_s...]
where the time goes in v3:
time: 21.6 us; the launch traced here: 21.4 us
  Pallas kernels  19.5 us (90%)
  between operations  1.29 us (6%)
  local copies, waits for them, and re-layouts  0.62 us (3%)
    pallas_call x1, Pallas kernels, shards(): pl.pallas_call(functools.partial(wake_kernel, nrows, ncols, tiles), out_s...  19.5 us
    slice x1, local copies, waits for them, and re-layouts, shards(): return (sums[0:3], sums[3:6])  0.62 us

profile of v3, /device:TPU:0, one launch (start us, length us, event | category | flops | bytes accessed | tf_op | source)
XLA Modules:
  0.0 21.4 jit_solution(2234175200351899719)
XLA Ops:
  1.3 19.5 %wake.1 = f32[6,1024]{1,0:T(8,128)S(1)} custom-call(s32[1]{0:T(128)S(6)} %copy.9.count_in, s32[8]{0:T(128)} %counts_in.1, s32[2,64]{1,0:T(2,128)} %slots_in.1, f32[3,1024]{1,0:T(4,128)} %pos_in.1, f32[3,1024]{1,0:T(4,128)} %strg_in.1, f32[8,128]{1,0:T(8,128)} %bitcast.2, s32[8,128]{1,0:T(8,128)} %bitcast.3), custom_call_target="tpu_custom_call" | custom-call | tf_op jit(solution)/shard_map/wake/pallas_call | solution.py:332
  20.7 0.6 %fusion = (f32[3,1024]{1,0:T(4,128)}, f32[3,1024]{1,0:T(4,128)}) fusion(f32[6,1024]{1,0:T(8,128)S(1)} %wake.1), kind=kLoop, calls=%fused_computation | loop fusion | bytes 49152 | tf_op jit(solution)/shard_map/slice | solution.py:377
